TPU v7x, 256 devices: a whole 4x4x8 slice. The times are simulated.
256 devices in a mesh: gx: 16 (over y, x), gy: 16 (over z, core).
Axes of the slice: x: 4, y: 4, z: 8, core: 2. Of those that a mesh axis runs over, the one named last changes fastest.
Arguments:
- amplitudes: bfloat16 [6, 16, 2048, 2048], P(None, 'gy', 'gx'), may hold values from -6 to 6
- coulomb: bfloat16 [16, 2048, 1, 2048], P('gy', 'gx'), may hold values from -0.03125 to 0.03125
- exchange_ints: bfloat16 [16, 2048, 1, 2048], P('gy', 'gx'), may hold values from -0.03125 to 0.03125
- block_sizes: int32 [4], replicated, may hold values from 64 to 1024, as said below
- occ_irreps: int32 [250], replicated, may hold values from 0 to 3
- tile_i: int32 [6], replicated, may hold values from 0 to 249
- tile_j: int32 [1], replicated, may hold values from 0 to 249
Outputs:
- residual: float32 [6, 2048, 1, 2048], P(None, 'gx', None, 'gy')
Inputs may be any that keep to these rules, and one draw needn't show every extreme that they name: `block_sizes`: the sizes sum to 2048; one irrep has exactly 64, and one has exactly half of 2048, rounded down.
All inputs are finite; a program needn't handle non-finite values.
Results may differ from a plain program's by a relative error of at most 0.0003.
Values may be sent and summed in bfloat16 or wider, within the bound.
A program may use at most 128 MiB of HBM per device.

v0:
```python
import jax
import jax.numpy as jnp
from jax import lax
from jax.sharding import PartitionSpec as P


def irrep_of(index, block_sizes):
    block_ends = jnp.cumsum(block_sizes)
    return jnp.sum((index[:, None] >= block_ends[None, :-1]).astype(jnp.int32), axis=1)


def occupied_irrep(tile_ids, occ_irreps):
    orbitals = jnp.arange(occ_irreps.shape[0], dtype=jnp.int32)
    onehot = (tile_ids[:, None] == orbitals[None, :]).astype(jnp.int32)
    return jnp.sum(onehot * occ_irreps[None, :], axis=1)


def swap_amplitudes(amplitudes):
    return lax.all_to_all(amplitudes, "gx", split_axis=3, concat_axis=2, tiled=True)


def direct_term(amplitudes, coul_piece):
    doubled = coul_piece * jnp.asarray(2.0, coul_piece.dtype)
    return jnp.einsum("ikac,kcjb->iajb", amplitudes, doubled, preferred_element_type=jnp.float32)


def swapped_term(total, swapped, exch_piece):
    return total - jnp.einsum(
        "ikca,kcjb->iajb", swapped, exch_piece, preferred_element_type=jnp.float32
    )


def per_device(amplitudes, coulomb, exchange_ints, block_sizes, occ_irreps, tile_i, tile_j):
    local_rows = amplitudes.shape[2]
    swapped = swap_amplitudes(amplitudes)
    total = direct_term(amplitudes, lax.all_gather(coulomb, "gx", axis=1, tiled=True))
    cycle = swapped_term(total, swapped, lax.all_gather(exchange_ints, "gx", axis=1, tiled=True))
    summed = lax.psum_scatter(cycle, "gy", scatter_dimension=3, tiled=True)
    cols_local = summed.shape[3]
    rows_global = lax.axis_index("gx") * local_rows + jnp.arange(local_rows, dtype=jnp.int32)
    cols_global = lax.axis_index("gy") * cols_local + jnp.arange(cols_local, dtype=jnp.int32)
    irrep_rows = irrep_of(rows_global, block_sizes)
    irrep_cols = irrep_of(cols_global, block_sizes)
    pair_irrep = jnp.bitwise_xor(
        occupied_irrep(tile_i, occ_irreps)[:, None], occupied_irrep(tile_j, occ_irreps)[None, :]
    )
    allowed = (
        jnp.bitwise_xor(irrep_rows[None, :, None, None], irrep_cols[None, None, None, :])
        == pair_irrep[:, None, :, None]
    )
    return jnp.where(allowed, summed, jnp.float32(0.0))


def solution(mesh):
    return jax.shard_map(
        per_device,
        mesh=mesh,
        in_specs=(
            P(None, "gy", "gx", None),
            P("gy", "gx", None, None),
            P("gy", "gx", None, None),
            P(),
            P(),
            P(),
            P(),
        ),
        out_specs=P(None, "gx", None, "gy"),
        check_vma=False,
    )
```

profile of v0, /device:TPU:1, one launch (start us, length us, event | category | flops | bytes accessed | tf_op | source)
XLA Modules:
  0.0 298.4 jit_solution(16797091909529455831)
XLA Ops:
  6.5 0.0 all-gather.5.cloned.1.call-start
  6.5 0.7 all-gather.5.cloned.1.call-update
  7.3 0.0 all-gather.3.cloned.1.call-start
  7.3 2.0 copy.29
  9.3 0.0 all-gather.3.cloned.1.call-update
  9.4 0.0 reduce-scatter.2.cloned.1.call-start
  9.4 6.3 %copy.30 = bf16[6,1,128,2048]{2,0,1,3:T(8,128)(2,1)} copy(bf16[6,1,128,2048]{3,2,1,0:T(8,128)(2,1)} %param.7) | data formatting | bytes 6291456 | tf_op args[0]
  15.7 65.8 %all_to_all.15 = bf16[6,1,128,2048]{2,0,1,3:T(8,128)(2,1)S(1)} all-to-all(bf16[6,1,128,2048]{2,0,1,3:T(8,128)(2,1)} %copy.30), channel_id=1, replica_groups=mesh['gx'=16,'gy'=16] {'gx'}, dimensions={3} | all-to-all | bytes 6291456 | tf_op jit(solution)/shard_map/all_to_all | solution.py:19
  81.6 0.4 copy.31
  82.0 2.0 copy.32
  84.0 3.4 %reshape.91 = bf16[6,2048,128]{1,2,0:T(8,128)(2,1)} reshape(bf16[6,1,16,128,128]{3,2,4,0,1:T(8,128)(2,1)S(1)} %copy.32) | data formatting | bytes 6291456 | tf_op jit(solution)/shard_map/reshape.13
  87.5 0.0 copy-start
  87.5 41.9 %all-gather.5.cloned.1.call-done = bf16[1,2048,1,2048]{3,1,2,0:T(8,128)(2,1)} async-done(((bf16[1,128,1,2048]{3,1,2,0:T(8,128)(2,1)}), bf16[1,2048,1,2048]{3,1,2,0:T(8,128)(2,1)}) %all-gather.5.cloned.1.call-update) | async-done | bytes 8388624 | tf_op jit(solution)/shard_map/all_gather | solution.py:37
  129.4 11.8 %fusion = f32[6,128,2048]{1,2,0:T(8,128)} fusion(bf16[6,2048,128]{1,2,0:T(8,128)(2,1)} %reshape.91, bf16[1,2048,1,2048]{3,1,2,0:T(8,128)(2,1)} %all-gather.5.cloned.1.call-done), kind=kOutput, calls=%fused_computation | convolution fusion | flops 6442450944 | bytes 17825792 | tf_op jit(solution)/shard_map/ikca,kcjb->iajb/dot_general | solution.py:28
  141.2 72.8 %all-gather.3.cloned.1.call-done = bf16[1,2048,1,2048]{1,3,2,0:T(8,128)(2,1)} async-done(((bf16[1,128,1,2048]{1,3,2,0:T(8,128)(2,1)}), bf16[1,2048,1,2048]{1,3,2,0:T(8,128)(2,1)}) %all-gather.3.cloned.1.call-update) | async-done | bytes 8388624 | tf_op jit(solution)/shard_map/all_gather | solution.py:36
  214.1 0.0 copy-done
  214.1 11.7 %fusion.5 = f32[6,128,1,2048]{1,3,0,2:T(8,128)} fusion(f32[6,128,2048]{1,2,0:T(8,128)} %fusion, bf16[1,2048,1,2048]{1,3,2,0:T(8,128)(2,1)} %all-gather.3.cloned.1.call-done, bf16[6,1,128,2048]{3,2,1,0:T(8,128)(2,1)S(1)} %copy-done), kind=kOutput, calls=%fused_computation.6 | convolution fusion | flops 6460801024 | bytes 24117248 | tf_op jit(solution)/shard_map/ikac,kcjb->iajb/dot_general | solution.py:24
  225.8 0.0 copy-start.3
  225.8 0.0 copy-start.1
  225.8 0.0 copy-start.2
  225.8 0.0 reduce-scatter.2.cloned.1.call-update
  226.5 0.0 copy-done.3
  226.5 0.2 reduce-window.4
  226.7 0.0 copy-done.1
  226.7 0.7 fusion.10
  227.4 0.0 copy-done.2
  227.4 0.2 select_reduce_fusion
  227.6 0.1 convert_reduce_fusion.1
  227.7 0.6 broadcast_xor_fusion.1
  228.3 0.1 broadcast_xor_fusion
  228.4 61.4 %reduce-scatter.2.cloned.1.call-done = f32[6,128,1,128]{1,3,0,2:T(8,128)} async-done(((f32[6,128,1,2048]{1,3,0,2:T(8,128)}), f32[6,128,1,128]{1,3,0,2:T(8,128)}) %reduce-scatter.2.cloned.1.call-update) | async-done | bytes 393232 | tf_op jit(solution)/shard_map/reduce_scatter | solution.py:38
  289.8 1.1 compare_select_fusion
  290.9 1.0 copy.34
  (2 shorter events, 0.0 us)
Async XLA Ops:
  6.5 122.9 %all-gather.5.cloned.1.call-start = ((), (), s32[]{:S(2)}) async-start(), calls=%async_computation.3 | async-start | bytes 8912896 | tf_op jit(solution)/shard_map/all_gather | solution.py:37
  7.3 206.8 %all-gather.3.cloned.1.call-start = ((), (), s32[]{:S(2)}) async-start(), calls=%async_computation.2 | async-start | bytes 8912896 | tf_op jit(solution)/shard_map/all_gather | solution.py:36
  9.4 280.4 %reduce-scatter.2.cloned.1.call-start = ((), (), s32[]{:S(2)}) async-start(), calls=%async_computation.4 | async-start | bytes 6684672 | tf_op jit(solution)/shard_map/reduce_scatter | solution.py:38
  87.5 126.6 %copy-start = (bf16[6,1,128,2048]{3,2,1,0:T(8,128)(2,1)S(1)}, bf16[6,1,128,2048]{3,2,1,0:T(8,128)(2,1)}, u32[]{:S(2)}) copy-start(bf16[6,1,128,2048]{3,2,1,0:T(8,128)(2,1)} %param.7) | copy-start | bytes 9437188
  225.8 0.7 copy-start.3
  225.8 0.9 copy-start.1
  225.8 1.6 copy-start.2
Sparse Core Ops, SparseCore 0:
  9.8 119.5 all-gather.4
  131.8 82.2 all-gather.2
  225.9 63.8 reduce-scatter.1
where the time goes:
time: 301 us; the launch traced here: 298 us
  waiting for transfers between devices  177 us (59%)
  blocking collectives  65.8 us (22%)
  matrix products  23.6 us (8%)
  local copies, waits for them, and re-layouts  15.3 us (5%)
  between operations  13.8 us (5%)
    all_gather x1, waiting for transfers between devices, per_device(): lax.all_gather(coulomb, 'gx', axis=1, tiled=True)  72.8 us
    all_to_all x1, blocking collectives, swap_amplitudes(): lax.all_to_all(amplitudes, 'gx', split_axis=3, concat_axis=2, tiled=True)  65.8 us
    reduce_scatter x1, waiting for transfers between devices, per_device(): summed = lax.psum_scatter(cycle, 'gy', scatter_dimension=3, tiled=True)  61.4 us
    all_gather x1, waiting for transfers between devices, per_device(): lax.all_gather(exchange_ints, 'gx', axis=1, tiled=True)  41.9 us
    dot_general x1, matrix products, swapped_term(): jnp.einsum('ikca,kcjb->iajb', swapped, exch_piece, preferred_element_type...  11.8 us
    dot_general x1, matrix products, direct_term(): jnp.einsum('ikac,kcjb->iajb', amplitudes, doubled, preferred_element_type...  11.7 us
    unnamed x10, local copies, waits for them, and re-layouts  8.38 us
  transfers between devices with their start and end apart: 3, of which 3 were waited for; matrix products, arithmetic and copies ran while one was open for 9% of the time, Pallas kernels for 0%

commit v1 on v0

v1 whole, which is shorter than its diff:
```python
import jax
import jax.numpy as jnp
from jax import lax
from jax.experimental import pallas as pl
from jax.experimental.pallas import tpu as pltpu
from jax.sharding import PartitionSpec as P

MESH = pl.DeviceIdType.MESH
NY, NX, NZ = 4, 4, 8
NIRREP = 4
NS = 3
BLK = 128
GRP = NY * BLK
TILE = 256
SUB = 8
ROWS = GRP // SUB
WIN = 33
LAST = ROWS - WIN
TOP = 17
F32 = jnp.float32


def step_tile(step):
    half = lax.div(step + 1, 2)
    return 4 + half * (1 - 2 * lax.rem(step, 2))


def kernel(amp, coul, exch, sizes, occ, tile_i, tile_j, out, left, raw, right, dense, part, zin, wide, yout, yin,
           t1_recv, t2_recv, t_send, w_recv, w_send, c_recv, c_send, z_recv, z_send, y_recv, y_send):
    gx, gy = lax.axis_index("gx"), lax.axis_index("gy")
    y, x = lax.div(gx, NX), lax.rem(gx, NX)
    z, core = lax.div(gy, 2), lax.rem(gy, 2)

    def device(dy=0, dx=0, dz=0, dc=0):
        y2, x2 = lax.rem(y + dy, NY), lax.rem(x + dx, NX)
        z2, core2 = lax.rem(z + dz, NZ), lax.rem(core + dc, 2)
        return (y2 * NX + x2, z2 * 2 + core2)

    barrier = pltpu.get_barrier_semaphore()
    partners = [dict(dy=dy, dc=dc) for dy in range(NY) for dc in range(2) if dy or dc]
    partners += [dict(dx=dx, dc=dc) for dx in range(1, NX) for dc in range(2)]
    partners += [dict(dz=1), dict(dz=NZ - 1)]
    for partner in partners:
        pl.semaphore_signal(barrier, inc=1, device_id=device(**partner), device_id_type=MESH)
    pl.semaphore_wait(barrier, len(partners))

    def loop(count, body, unroll=None):
        lax.fori_loop(0, count, lambda n, carry: (body(n), carry)[1], 0, unroll=unroll)

    def send_amplitudes(s):
        for dc in range(2):
            row = 3 * lax.rem(core + dc, 2) + s
            for dy in range(NY):
                y2 = lax.rem(y + dy, NY)
                src = amp.at[row, :, pl.ds(pl.multiple_of(GRP * y2, GRP), GRP)]
                dst = left.at[s, pl.ds(pl.multiple_of(BLK * y, BLK), BLK), pl.ds(pl.multiple_of(GRP * core, GRP), GRP)]
                if dy or dc:
                    pltpu.make_async_remote_copy(
                        src, dst, t_send.at[s], t1_recv.at[s], device_id=device(dy=dy, dc=dc), device_id_type=MESH
                    ).start()
                else:
                    pltpu.make_async_copy(src, dst, t1_recv.at[s]).start()
            for dx in range(NX):
                x2 = lax.rem(x + dx, NX)
                for y2 in range(NY):
                    src = amp.at[row, :, pl.ds(pl.multiple_of(GRP * y2 + BLK * x2, BLK), BLK)]
                    dst = raw.at[s, core, pl.ds(pl.multiple_of(BLK * x, BLK), BLK), pl.ds(BLK * y2, BLK)]
                    if dx or dc:
                        pltpu.make_async_remote_copy(
                            src, dst, t_send.at[s], t2_recv.at[s], device_id=device(dx=dx, dc=dc), device_id_type=MESH
                        ).start()
                    else:
                        pltpu.make_async_copy(src, dst, t2_recv.at[s]).start()

    def send_integrals(step):
        tile = lax.rem(z + step_tile(step), NZ)
        columns = pl.ds(pl.multiple_of(TILE * tile, TILE), TILE)
        for dx in range(NX):
            for term, ref in ((0, coul), (1, exch)):
                src, dst = ref.at[:, columns], right.at[step, term, core, x]
                if dx:
                    pltpu.make_async_remote_copy(
                        src, dst, w_send.at[step], w_recv.at[step], device_id=device(dx=dx), device_id_type=MESH
                    ).start()
                else:
                    pltpu.make_async_copy(src, dst, w_recv.at[step]).start()

    def wait_bytes(ref, sem):
        pltpu.make_async_copy(ref, ref, sem).wait()

    def take_amplitudes(s):
        wait_bytes(left.at[s, :, pl.ds(0, 2 * GRP)], t1_recv.at[s])
        wait_bytes(raw.at[s], t2_recv.at[s])
        for k in range(2):
            left[s, :, pl.ds((2 + k) * GRP, GRP)] = (raw[s, k] * jnp.asarray(-0.5, jnp.bfloat16)).T

    def share_integrals(step):
        return pltpu.make_async_remote_copy(
            right.at[step, :, core], right.at[step, :, core], c_send.at[step], c_recv.at[step],
            device_id=device(dc=1), device_id_type=MESH,
        )

    def take_integrals(step):
        wait_bytes(right.at[step, :, core], w_recv.at[step])
        share_integrals(step).start()
        wait_bytes(right.at[step, :, 1 - core], c_recv.at[step])

    first_end = sizes[0]
    second_end = first_end + sizes[1]
    third_end = second_end + sizes[2]

    def irrep(index):
        return (
            (index >= first_end).astype(jnp.int32)
            + (index >= second_end).astype(jnp.int32)
            + (index >= third_end).astype(jnp.int32)
        )

    def pair_irrep(i):
        return occ[tile_i[i]] ^ occ[tile_j[0]]

    def window(i, col_irrep):
        row_irrep = pair_irrep(i) ^ col_irrep
        begin = jnp.where(row_irrep > 0, sizes[0], 0) + jnp.where(row_irrep > 1, sizes[1], 0)
        begin = begin + jnp.where(row_irrep > 2, sizes[2], 0)
        block = lax.div(begin, GRP)
        local = block * BLK + jnp.clip(begin - block * GRP - BLK * x, 0, BLK)
        return jnp.minimum(lax.div(local, SUB), LAST)

    def columns_irrep(step):
        tile = lax.rem(z + step_tile(step), NZ)
        return irrep(TILE * tile + lax.broadcasted_iota(jnp.int32, (1, TILE), 1))

    def z_copy(s, step):
        up = lax.rem(step, 2)
        return pltpu.make_async_remote_copy(
            part.at[s, step], zin.at[s, step + 2], z_send.at[s, step], z_recv.at[s, step + 2],
            device_id=device(dz=up + (1 - up) * (NZ - 1)), device_id_type=MESH,
        )

    def z_first(s):
        upper, lower = pl.ds(0, TOP), pl.ds(TOP, WIN - TOP)
        return [
            pltpu.make_async_remote_copy(
                part.at[s, 0, upper], zin.at[s, 1, upper], z_send.at[s, 0], z_recv.at[s, 1],
                device_id=device(dz=1), device_id_type=MESH,
            ),
            pltpu.make_async_remote_copy(
                part.at[s, 0, lower], zin.at[s, 2, lower], z_send.at[s, 7], z_recv.at[s, 2],
                device_id=device(dz=NZ - 1), device_id_type=MESH,
            ),
        ]

    def y_copy(s, dy, dc):
        y2, core2 = lax.rem(y + dy, NY), lax.rem(core + dc, 2)
        src, dst = yout.at[s, 2 * y2 + core2], yin.at[3 * core + s, y]
        if dy or dc:
            return pltpu.make_async_remote_copy(
                src, dst, y_send.at[s], y_recv.at[3 * core + s], device_id=device(dy=dy, dc=dc), device_id_type=MESH
            )
        return pltpu.make_async_copy(src, dst, y_recv.at[3 * core + s])

    def compute(s, step):
        product = jnp.dot(left[s], right[step].reshape(4 * GRP, TILE), preferred_element_type=F32)
        dense[...] = product.reshape(ROWS, SUB, TILE)
        kinds = columns_irrep(step)
        begins = [window(3 * core + s, kind) for kind in range(NIRREP)]

        def pack(row):
            packed = dense[begins[0] + row]
            for kind in range(1, NIRREP):
                packed = jnp.where(kinds == kind, dense[begins[kind] + row], packed)
            part[s, step, row] = packed

        loop(WIN, pack, unroll=True)

    def pass_on(s, step):
        @pl.when(step == 0)
        def _():
            for copy in z_first(s):
                copy.start()

        @pl.when(step == 1)
        def _():
            rows = pl.ds(0, TOP)
            wait_bytes(zin.at[s, 1, rows], z_recv.at[s, 1])
            part[s, 1, rows] += zin[s, 1, rows]

        @pl.when(step == 2)
        def _():
            rows = pl.ds(TOP, WIN - TOP)
            wait_bytes(zin.at[s, 2, rows], z_recv.at[s, 2])
            part[s, 2, rows] += zin[s, 2, rows]

        @pl.when((step > 2) & (step < 7))
        def _():
            wait_bytes(zin.at[s, step], z_recv.at[s, step])
            part[s, step] += zin[s, step]

        @pl.when((step > 0) & (step < 7))
        def _():
            z_copy(s, step).start()

    def finish(s):
        wait_bytes(zin.at[s, 7], z_recv.at[s, 7])
        wait_bytes(zin.at[s, 8], z_recv.at[s, 8])
        wide[pl.ds(LAST, WIN)] = part[s, 7] + zin[s, 7] + zin[s, 8]
        kinds = columns_irrep(7)
        begins = [LAST - window(3 * core + s, kind) for kind in range(NIRREP)]
        for block in range(NY):

            def unpack(row):
                rows = wide[begins[0] + block * (BLK // SUB) + row]
                for kind in range(1, NIRREP):
                    rows = jnp.where(kinds == kind, wide[begins[kind] + block * (BLK // SUB) + row], rows)
                for half in range(2):
                    yout[s, 2 * block + half, row] = rows[:, half * BLK:(half + 1) * BLK]

            loop(BLK // SUB, unpack, unroll=True)
        for dc in range(2):
            for dy in range(NY):
                y_copy(s, dy, dc).start()

    def write(i):
        wait_bytes(yin.at[i], y_recv.at[i])
        total = 2.0 * (yin[i, 0] + yin[i, 1] + yin[i, 2] + yin[i, 3]).reshape(BLK, BLK)
        rows = irrep(BLK * gx + lax.broadcasted_iota(jnp.int32, (BLK, 1), 0))
        columns = irrep(BLK * gy + lax.broadcasted_iota(jnp.int32, (1, BLK), 1))
        out[i] = jnp.where((rows ^ columns) == pair_irrep(i), total, 0.0)

    loop(NS, send_amplitudes)
    loop(NZ, send_integrals)
    wide[pl.ds(0, LAST)] = jnp.zeros((LAST, SUB, TILE), F32)
    wide[pl.ds(ROWS, LAST)] = jnp.zeros((LAST, SUB, TILE), F32)
    loop(NS, take_amplitudes)

    def one(n):
        step, s = lax.div(n, NS), lax.rem(n, NS)

        @pl.when(s == 0)
        def _():
            take_integrals(step)

        compute(s, step)
        pass_on(s, step)

    loop(NZ * NS, one)
    loop(NS, finish)
    loop(2 * NS, lambda n: write(3 * lax.rem(n, 2) + lax.div(n, 2)))

    def drain(s):
        wait_bytes(left.at[s, pl.ds(0, 448), :], t_send.at[s])
        for copy in z_first(s):
            copy.wait_send()
        loop(6, lambda step: z_copy(s, step + 1).wait_send())
        wait_bytes(yout.at[s, pl.ds(0, 7)], y_send.at[s])

    loop(NS, drain)

    def drain_integrals(step):
        wait_bytes(right.at[step, 0, :, pl.ds(0, 3)], w_send.at[step])
        share_integrals(step).wait_send()

    loop(NZ, drain_integrals)


def per_device(amplitudes, coulomb, exchange_ints, block_sizes, occ_irreps, tile_i, tile_j):
    depth, columns = coulomb.shape[1], coulomb.shape[3]
    count = amplitudes.shape[0]
    anywhere, scalars = pl.BlockSpec(memory_space=pl.ANY), pl.BlockSpec(memory_space=pltpu.SMEM)
    dma = pltpu.SemaphoreType.DMA
    residual = pl.pallas_call(
        kernel,
        out_shape=jax.ShapeDtypeStruct((count, BLK, BLK), F32),
        in_specs=[anywhere] * 3 + [scalars] * 4,
        out_specs=pl.BlockSpec(memory_space=pltpu.VMEM),
        scratch_shapes=[
            pltpu.VMEM((NS, GRP, 4 * GRP), jnp.bfloat16),
            pltpu.VMEM((NS, 2, GRP, GRP), jnp.bfloat16),
            pltpu.VMEM((NZ, 2, 2, NX, BLK, TILE), jnp.bfloat16),
            pltpu.VMEM((ROWS, SUB, TILE), F32),
            pltpu.VMEM((NS, NZ, WIN, SUB, TILE), F32),
            pltpu.VMEM((NS, NZ + 1, WIN, SUB, TILE), F32),
            pltpu.VMEM((ROWS + LAST, SUB, TILE), F32),
            pltpu.VMEM((NS, 2 * NY, BLK // SUB, SUB, BLK), F32),
            pltpu.VMEM((2 * NS, NY, BLK // SUB, SUB, BLK), F32),
            dma((NS,)), dma((NS,)), dma((NS,)),
            dma((NZ,)), dma((NZ,)), dma((NZ,)), dma((NZ,)),
            dma((NS, NZ + 1)), dma((NS, NZ)),
            dma((2 * NS,)), dma((NS,)),
        ],
        compiler_params=pltpu.CompilerParams(
            collective_id=0, has_side_effects=True, vmem_limit_bytes=56 * 1024 * 1024
        ),
        cost_estimate=pl.CostEstimate(flops=12900000000, bytes_accessed=5000000, transcendentals=0),
    )(
        amplitudes.reshape(count, BLK, columns),
        coulomb.reshape(depth, columns),
        exchange_ints.reshape(depth, columns),
        block_sizes, occ_irreps, tile_i, tile_j,
    )
    return residual.reshape(count, BLK, 1, BLK)


def solution(mesh):
    return jax.shard_map(
        per_device,
        mesh=mesh,
        in_specs=(
            P(None, "gy", "gx", None),
            P("gy", "gx", None, None),
            P("gy", "gx", None, None),
            P(),
            P(),
            P(),
            P(),
        ),
        out_specs=P(None, "gx", None, "gy"),
        check_vma=False,
    )
```

time: 301 us -> 135 us (0.45)
  waiting for transfers between devices: 177 us -> 0 us
  Pallas kernels: 0 us -> 132 us
  blocking collectives: 65.8 us -> 0 us
  matrix products: 23.6 us -> 0 us
  local copies, waits for them, and re-layouts: 15.3 us -> 1.77 us
  between operations: 13.8 us -> 0.66 us
    pallas_call x0 -> x1, Pallas kernels: none -> 132 us  [per_device(): pl.pallas_call(kernel, out_shape=jax.ShapeDtypeStruct((count, BLK, BLK),...]
    all_gather x2 -> x0, waiting for transfers between devices: 115 us -> none  [the longest x1 72.8 us: per_device(): lax.all_gather(coulomb, 'gx', axis=1, tiled=True)]
    all_to_all x1 -> x0, blocking collectives: 65.8 us -> none  [swap_amplitudes(): lax.all_to_all(amplitudes, 'gx', split_axis=3, concat_axis=2, tiled=True)]
    reduce_scatter x1 -> x0, waiting for transfers between devices: 61.4 us -> none  [per_device(): summed = lax.psum_scatter(cycle, 'gy', scatter_dimension=3, tiled=True)]
    dot_general x2 -> x0, matrix products: 23.6 us -> none  [the longest x1 11.8 us: swapped_term(): jnp.einsum('ikca,kcjb->iajb', swapped, exch_piece, preferred_element_type...]
    unnamed x10 -> x1, local copies, waits for them, and re-layouts: 8.38 us -> 1.77 us
    another operation x1 -> x0, local copies, waits for them, and re-layouts: 3.43 us -> none
  transfers between devices with their start and end apart: 3 -> 0, of which waited for: 3 -> 0; matrix products, arithmetic and copies ran while one was open for 9% -> 0% of each run, Pallas kernels for 0% -> 0%
where the time goes in v1:
time: 135 us
  Pallas kernels  132 us (98%)
  local copies, waits for them, and re-layouts  1.77 us (1%)
    pallas_call x1, Pallas kernels, per_device(): pl.pallas_call(kernel, out_shape=jax.ShapeDtypeStruct((count, BLK, BLK),...  132 us

profile of v1, /device:TPU:1, one launch (start us, length us, event | category | flops | bytes accessed | tf_op | source)
XLA Modules:
  0.0 134.7 jit_solution(1271258151082218060)
XLA Ops:
  0.7 132.3 %shard_map.73 = f32[6,128,128]{2,1,0:T(8,128)} custom-call(bf16[6,128,2048]{2,1,0:T(8,128)(2,1)} %bitcast.7, bf16[128,2048]{1,0:T(8,128)(2,1)} %bitcast.8, bf16[128,2048]{1,0:T(8,128)(2,1)} %bitcast.9, s32[4]{0:T(128)} %sizes.1, s32[250]{0:T(256)} %occ.1, s32[6]{0:T(128)} %tile_i.1, s32[1]{0:T(128)S(6)} %copy.10.tile_j), custom_call_target="tpu_custom_call" | custom-call | flops 12899999744 | bytes 5000000 | tf_op jit(solution)/shard_map/pallas_call | solution.py:272
  133.0 1.8 %copy.11 = f32[6,128,1,128]{3,2,1,0:T(1,128)} copy(f32[6,128,1,128]{3,2,1,0:T(1,128)} %bitcast.6) | data formatting | bytes 786432

commit v2 on v1

--- a/solution.py
+++ b/solution.py
@@ -16,8 +16,30 @@
 ROWS = GRP // SUB
 WIN = 33
 LAST = ROWS - WIN
-TOP = 17
+SHARE, QUARTER = 8, 9
+UPPER, LOWER = pl.ds(0, 17), pl.ds(17, 16)
+Q_UPPER, Q_LOWER = pl.ds(0, 5), pl.ds(5, 4)
 F32 = jnp.float32
+
+
+def make_plan():
+    units = sorted(
+        [(s, step) for s in range(NS) for step in range(NZ)], key=lambda unit: ((unit[1] + 1) // 2, unit[0], unit[1])
+    )
+    before = [("amp", s) for s in range(NS)] + [("own", step) for step in range(NZ)]
+    early = [[] for _ in units]
+    for s in range(NS):
+        early[units.index((s, 0))] += [("got", s)]
+    for step in range(NZ):
+        early[units.index((0, step))] += [("share", step), ("have", step)]
+    after = [("finish", 0), ("finish", 1)]
+    for step in range(NZ):
+        place = units.index((NS - 1, step)) + 6
+        (early[place] if place < len(units) else after).append(("quarter", step))
+    return units, before, early, after
+
+
+UNITS, BEFORE, EARLY, AFTER = make_plan()
 
 
 def step_tile(step):
@@ -26,7 +48,9 @@
 
 
 def kernel(amp, coul, exch, sizes, occ, tile_i, tile_j, out, left, raw, right, dense, part, zin, wide, yout, yin,
-           t1_recv, t2_recv, t_send, w_recv, w_send, c_recv, c_send, z_recv, z_send, y_recv, y_send):
+           split, quarter, qin, gout, gin, narrow, flat,
+           t1_recv, t2_recv, t_send, w_recv, w_send, c_recv, c_send, z_recv, z_send, y_recv, y_send,
+           s_recv, s_send, q_recv, q_send, g_recv, g_send):
     gx, gy = lax.axis_index("gx"), lax.axis_index("gy")
     y, x = lax.div(gx, NX), lax.rem(gx, NX)
     z, core = lax.div(gy, 2), lax.rem(gy, 2)
@@ -75,7 +99,7 @@
     def send_integrals(step):
         tile = lax.rem(z + step_tile(step), NZ)
         columns = pl.ds(pl.multiple_of(TILE * tile, TILE), TILE)
-        for dx in range(NX):
+        for dx in (1, 3, 2, 0):
             for term, ref in ((0, coul), (1, exch)):
                 src, dst = ref.at[:, columns], right.at[step, term, core, x]
                 if dx:
@@ -103,6 +127,8 @@
     def take_integrals(step):
         wait_bytes(right.at[step, :, core], w_recv.at[step])
         share_integrals(step).start()
+
+    def take_shared(step):
         wait_bytes(right.at[step, :, 1 - core], c_recv.at[step])
 
     first_end = sizes[0]
@@ -139,17 +165,46 @@
         )
 
     def z_first(s):
-        upper, lower = pl.ds(0, TOP), pl.ds(TOP, WIN - TOP)
         return [
             pltpu.make_async_remote_copy(
-                part.at[s, 0, upper], zin.at[s, 1, upper], z_send.at[s, 0], z_recv.at[s, 1],
-                device_id=device(dz=1), device_id_type=MESH,
-            ),
+                part.at[s, 0, rows], zin.at[s, slot, rows], z_send.at[s, sem], z_recv.at[s, slot],
+                device_id=device(dz=dz), device_id_type=MESH,
+            )
+            for rows, slot, sem, dz in ((UPPER, 1, 0, 1), (LOWER, 2, 7, NZ - 1))
+        ]
+
+    def q_copy(step):
+        up = lax.rem(step, 2)
+        return pltpu.make_async_remote_copy(
+            quarter.at[step], qin.at[step + 2], q_send.at[step], q_recv.at[step + 2],
+            device_id=device(dz=up + (1 - up) * (NZ - 1)), device_id_type=MESH,
+        )
+
+    def q_first():
+        return [
             pltpu.make_async_remote_copy(
-                part.at[s, 0, lower], zin.at[s, 2, lower], z_send.at[s, 7], z_recv.at[s, 2],
-                device_id=device(dz=NZ - 1), device_id_type=MESH,
-            ),
+                quarter.at[0, rows], qin.at[slot, rows], q_send.at[sem], q_recv.at[slot],
+                device_id=device(dz=dz), device_id_type=MESH,
+            )
+            for rows, slot, sem, dz in ((Q_UPPER, 1, 0, 1), (Q_LOWER, 2, 7, NZ - 1))
         ]
+
+    def split_rows(step):
+        for dy in (1, 3, 2):
+            y2 = lax.rem(y + dy, NY)
+            pltpu.make_async_remote_copy(
+                part.at[NS - 1, step, pl.ds(SHARE * y2, QUARTER)], split.at[step, y], s_send.at[step], s_recv.at[step],
+                device_id=device(dy=dy), device_id_type=MESH,
+            ).start()
+
+    def g_copy(dy, dc):
+        core2 = lax.rem(core + dc, 2)
+        src, dst = gout.at[core2], gin.at[NY * core + y]
+        if dy or dc:
+            return pltpu.make_async_remote_copy(
+                src, dst, g_send, g_recv.at[core], device_id=device(dy=dy, dc=dc), device_id_type=MESH
+            )
+        return pltpu.make_async_copy(src, dst, g_recv.at[core])
 
     def y_copy(s, dy, dc):
         y2, core2 = lax.rem(y + dy, NY), lax.rem(core + dc, 2)
@@ -180,17 +235,12 @@
             for copy in z_first(s):
                 copy.start()
 
-        @pl.when(step == 1)
-        def _():
-            rows = pl.ds(0, TOP)
-            wait_bytes(zin.at[s, 1, rows], z_recv.at[s, 1])
-            part[s, 1, rows] += zin[s, 1, rows]
-
-        @pl.when(step == 2)
-        def _():
-            rows = pl.ds(TOP, WIN - TOP)
-            wait_bytes(zin.at[s, 2, rows], z_recv.at[s, 2])
-            part[s, 2, rows] += zin[s, 2, rows]
+        for place, rows in ((1, UPPER), (2, LOWER)):
+
+            @pl.when(step == place)
+            def _():
+                wait_bytes(zin.at[s, place, rows], z_recv.at[s, place])
+                part[s, place, rows] += zin[s, place, rows]
 
         @pl.when((step > 2) & (step < 7))
         def _():
@@ -200,6 +250,29 @@
         @pl.when((step > 0) & (step < 7))
         def _():
             z_copy(s, step).start()
+
+    def pass_quarter(step):
+        wait_bytes(split.at[step, pl.ds(0, NY - 1)], s_recv.at[step])
+        total = part[NS - 1, step, pl.ds(SHARE * y, QUARTER)]
+        for dy in range(1, NY):
+            total = total + split[step, lax.rem(y + dy, NY)]
+        quarter[step] = total
+        if step == 0:
+            for copy in q_first():
+                copy.start()
+            return
+        for slot in (7, 8) if step == 7 else (step,):
+            rows = {1: Q_UPPER, 2: Q_LOWER}.get(slot, pl.ds(0, QUARTER))
+            wait_bytes(qin.at[slot, rows], q_recv.at[slot])
+            quarter[step, rows] += qin[slot, rows]
+        if step < 7:
+            q_copy(step).start()
+            return
+        for half in range(2):
+            gout[half] = quarter[7, :, :, pl.ds(half * BLK, BLK)]
+        for dc in range(2):
+            for dy in range(NY):
+                g_copy(dy, dc).start()
 
     def finish(s):
         wait_bytes(zin.at[s, 7], z_recv.at[s, 7])
@@ -221,47 +294,99 @@
             for dy in range(NY):
                 y_copy(s, dy, dc).start()
 
+    def mask(i, total):
+        rows = irrep(BLK * gx + lax.broadcasted_iota(jnp.int32, (BLK, 1), 0))
+        columns = irrep(BLK * gy + lax.broadcasted_iota(jnp.int32, (1, BLK), 1))
+        return jnp.where((rows ^ columns) == pair_irrep(i), total, 0.0)
+
+    def write_gathered(g):
+        i = NS * g + NS - 1
+        wait_bytes(gin.at[pl.ds(NY * g, NY)], g_recv.at[g])
+        for block in range(NY):
+            narrow[pl.ds(LAST + SHARE * block, QUARTER)] = gin[NY * g + block]
+        kinds = irrep(BLK * gy + lax.broadcasted_iota(jnp.int32, (1, BLK), 1))
+        begins = [LAST - window(i, kind) + y * (BLK // SUB) for kind in range(NIRREP)]
+
+        def unpack(row):
+            rows = narrow[begins[0] + row]
+            for kind in range(1, NIRREP):
+                rows = jnp.where(kinds == kind, narrow[begins[kind] + row], rows)
+            flat[row] = rows
+
+        loop(BLK // SUB, unpack, unroll=True)
+        out[i] = mask(i, 2.0 * flat[...].reshape(BLK, BLK))
+
     def write(i):
         wait_bytes(yin.at[i], y_recv.at[i])
         total = 2.0 * (yin[i, 0] + yin[i, 1] + yin[i, 2] + yin[i, 3]).reshape(BLK, BLK)
-        rows = irrep(BLK * gx + lax.broadcasted_iota(jnp.int32, (BLK, 1), 0))
-        columns = irrep(BLK * gy + lax.broadcasted_iota(jnp.int32, (1, BLK), 1))
-        out[i] = jnp.where((rows ^ columns) == pair_irrep(i), total, 0.0)
-
-    loop(NS, send_amplitudes)
-    loop(NZ, send_integrals)
-    wide[pl.ds(0, LAST)] = jnp.zeros((LAST, SUB, TILE), F32)
-    wide[pl.ds(ROWS, LAST)] = jnp.zeros((LAST, SUB, TILE), F32)
-    loop(NS, take_amplitudes)
+        out[i] = mask(i, total)
+
+    actions = dict(
+        amp=send_amplitudes, own=send_integrals, got=take_amplitudes, share=take_integrals, have=take_shared,
+        quarter=pass_quarter, finish=finish,
+    )
+
+    def look_up(n, values):
+        found = jnp.int32(values[0])
+        for place, value in enumerate(values[1:], 1):
+            found = jnp.where(n == place, value, found)
+        return found
+
+    def act(names):
+        for name, arg in names:
+            actions[name](arg)
+
+    for ref, size in ((wide, TILE), (narrow, BLK)):
+        ref[pl.ds(0, LAST)] = jnp.zeros((LAST, SUB, size), F32)
+        ref[pl.ds(ROWS, LAST)] = jnp.zeros((LAST, SUB, size), F32)
+    act(BEFORE)
 
     def one(n):
-        step, s = lax.div(n, NS), lax.rem(n, NS)
-
-        @pl.when(s == 0)
-        def _():
-            take_integrals(step)
-
+        for place in range(len(UNITS)):
+            if EARLY[place]:
+
+                @pl.when(n == place)
+                def _():
+                    act(EARLY[place])
+
+        s, step = look_up(n, [s for s, _ in UNITS]), look_up(n, [step for _, step in UNITS])
         compute(s, step)
-        pass_on(s, step)
-
-    loop(NZ * NS, one)
-    loop(NS, finish)
-    loop(2 * NS, lambda n: write(3 * lax.rem(n, 2) + lax.div(n, 2)))
+
+        @pl.when(s == NS - 1)
+        def _():
+            split_rows(step)
+
+        @pl.when(s < NS - 1)
+        def _():
+            pass_on(s, step)
+
+    loop(len(UNITS), one)
+    act(AFTER)
+    loop(4, lambda n: write(3 * lax.rem(n, 2) + lax.div(n, 2)))
+    loop(2, write_gathered)
 
     def drain(s):
         wait_bytes(left.at[s, pl.ds(0, 448), :], t_send.at[s])
-        for copy in z_first(s):
-            copy.wait_send()
-        loop(6, lambda step: z_copy(s, step + 1).wait_send())
-        wait_bytes(yout.at[s, pl.ds(0, 7)], y_send.at[s])
+
+        @pl.when(s < NS - 1)
+        def _():
+            for copy in z_first(s):
+                copy.wait_send()
+            loop(6, lambda step: z_copy(s, step + 1).wait_send())
+            wait_bytes(yout.at[s, pl.ds(0, 7)], y_send.at[s])
 
     loop(NS, drain)
 
-    def drain_integrals(step):
+    def drain_step(step):
         wait_bytes(right.at[step, 0, :, pl.ds(0, 3)], w_send.at[step])
         share_integrals(step).wait_send()
-
-    loop(NZ, drain_integrals)
+        wait_bytes(split.at[step, pl.ds(0, NY - 1)], s_send.at[step])
+
+    loop(NZ, drain_step)
+    for copy in q_first():
+        copy.wait_send()
+    loop(6, lambda step: q_copy(step + 1).wait_send())
+    wait_bytes(gin.at[pl.ds(0, 7)], g_send)
 
 
 def per_device(amplitudes, coulomb, exchange_ints, block_sizes, occ_irreps, tile_i, tile_j):
@@ -280,14 +405,23 @@
             pltpu.VMEM((NZ, 2, 2, NX, BLK, TILE), jnp.bfloat16),
             pltpu.VMEM((ROWS, SUB, TILE), F32),
             pltpu.VMEM((NS, NZ, WIN, SUB, TILE), F32),
-            pltpu.VMEM((NS, NZ + 1, WIN, SUB, TILE), F32),
+            pltpu.VMEM((NS - 1, NZ + 1, WIN, SUB, TILE), F32),
             pltpu.VMEM((ROWS + LAST, SUB, TILE), F32),
-            pltpu.VMEM((NS, 2 * NY, BLK // SUB, SUB, BLK), F32),
+            pltpu.VMEM((NS - 1, 2 * NY, BLK // SUB, SUB, BLK), F32),
             pltpu.VMEM((2 * NS, NY, BLK // SUB, SUB, BLK), F32),
+            pltpu.VMEM((NZ, NY, QUARTER, SUB, TILE), F32),
+            pltpu.VMEM((NZ, QUARTER, SUB, TILE), F32),
+            pltpu.VMEM((NZ + 1, QUARTER, SUB, TILE), F32),
+            pltpu.VMEM((2, QUARTER, SUB, BLK), F32),
+            pltpu.VMEM((2 * NY, QUARTER, SUB, BLK), F32),
+            pltpu.VMEM((ROWS + LAST, SUB, BLK), F32),
+            pltpu.VMEM((BLK // SUB, SUB, BLK), F32),
             dma((NS,)), dma((NS,)), dma((NS,)),
             dma((NZ,)), dma((NZ,)), dma((NZ,)), dma((NZ,)),
             dma((NS, NZ + 1)), dma((NS, NZ)),
             dma((2 * NS,)), dma((NS,)),
+            dma((NZ,)), dma((NZ,)), dma((NZ + 1,)), dma((NZ,)),
+            dma((2,)), dma,
         ],
         compiler_params=pltpu.CompilerParams(
             collective_id=0, has_side_effects=True, vmem_limit_bytes=56 * 1024 * 1024

time: 135 us -> 123 us (0.911)
  Pallas kernels: 132 us -> 120 us
    pallas_call x1, Pallas kernels: 132 us -> 120 us  [per_device(): pl.pallas_call(kernel, out_shape=jax.ShapeDtypeStruct((count, BLK, BLK),...]
where the time goes in v2:
time: 123 us
  Pallas kernels  120 us (98%)
  local copies, waits for them, and re-layouts  1.77 us (1%)
    pallas_call x1, Pallas kernels, per_device(): pl.pallas_call(kernel, out_shape=jax.ShapeDtypeStruct((count, BLK, BLK),...  120 us

profile of v2, /device:TPU:1, one launch (start us, length us, event | category | flops | bytes accessed | tf_op | source)
XLA Modules:
  0.0 122.8 jit_solution(8975355371400719104)
XLA Ops:
  0.7 120.4 %shard_map.73 = f32[6,128,128]{2,1,0:T(8,128)} custom-call(bf16[6,128,2048]{2,1,0:T(8,128)(2,1)} %bitcast.7, bf16[128,2048]{1,0:T(8,128)(2,1)} %bitcast.8, bf16[128,2048]{1,0:T(8,128)(2,1)} %bitcast.9, s32[4]{0:T(128)} %sizes.1, s32[250]{0:T(256)} %occ.1, s32[6]{0:T(128)} %tile_i.1, s32[1]{0:T(128)S(6)} %copy.10.tile_j), custom_call_target="tpu_custom_call" | custom-call | flops 12899999744 | bytes 5000000 | tf_op jit(solution)/shard_map/pallas_call | solution.py:397
  121.0 1.8 %copy.11 = f32[6,128,1,128]{3,2,1,0:T(1,128)} copy(f32[6,128,1,128]{3,2,1,0:T(1,128)} %bitcast.6) | data formatting | bytes 786432

commit v3 on v2

--- a/solution.py
+++ b/solution.py
@@ -34,7 +34,7 @@
         early[units.index((0, step))] += [("share", step), ("have", step)]
     after = [("finish", 0), ("finish", 1)]
     for step in range(NZ):
-        place = units.index((NS - 1, step)) + 6
+        place = units.index((NS - 1, step)) + 7
         (early[place] if place < len(units) else after).append(("quarter", step))
     return units, before, early, after
 
@@ -190,7 +190,7 @@
         ]
 
     def split_rows(step):
-        for dy in (1, 3, 2):
+        for dy in (2, 1, 3):
             y2 = lax.rem(y + dy, NY)
             pltpu.make_async_remote_copy(
                 part.at[NS - 1, step, pl.ds(SHARE * y2, QUARTER)], split.at[step, y], s_send.at[step], s_recv.at[step],
@@ -271,7 +271,7 @@
         for half in range(2):
             gout[half] = quarter[7, :, :, pl.ds(half * BLK, BLK)]
         for dc in range(2):
-            for dy in range(NY):
+            for dy in (2, 1, 3, 0):
                 g_copy(dy, dc).start()
 
     def finish(s):
@@ -291,7 +291,7 @@
 
             loop(BLK // SUB, unpack, unroll=True)
         for dc in range(2):
-            for dy in range(NY):
+            for dy in (2, 1, 3, 0):
                 y_copy(s, dy, dc).start()
 
     def mask(i, total):
@@ -336,10 +336,10 @@
         for name, arg in names:
             actions[name](arg)
 
+    act(BEFORE)
     for ref, size in ((wide, TILE), (narrow, BLK)):
         ref[pl.ds(0, LAST)] = jnp.zeros((LAST, SUB, size), F32)
         ref[pl.ds(ROWS, LAST)] = jnp.zeros((LAST, SUB, size), F32)
-    act(BEFORE)
 
     def one(n):
         for place in range(len(UNITS)):

time: 123 us -> 123 us (level)
  no operation moved by 1% of the time
where the time goes in v3:
time: 123 us; the launch traced here: 122 us
  Pallas kernels  120 us (98%)
  local copies, waits for them, and re-layouts  1.77 us (1%)
    pallas_call x1, Pallas kernels, per_device(): pl.pallas_call(kernel, out_shape=jax.ShapeDtypeStruct((count, BLK, BLK),...  120 us

profile of v3, /device:TPU:1, one launch (start us, length us, event | category | flops | bytes accessed | tf_op | source)
XLA Modules:
  0.0 122.4 jit_solution(15346877179409060613)
XLA Ops:
  0.7 120.0 %shard_map.73 = f32[6,128,128]{2,1,0:T(8,128)} custom-call(bf16[6,128,2048]{2,1,0:T(8,128)(2,1)} %bitcast.7, bf16[128,2048]{1,0:T(8,128)(2,1)} %bitcast.8, bf16[128,2048]{1,0:T(8,128)(2,1)} %bitcast.9, s32[4]{0:T(128)} %sizes.1, s32[250]{0:T(256)} %occ.1, s32[6]{0:T(128)} %tile_i.1, s32[1]{0:T(128)S(6)} %copy.10.tile_j), custom_call_target="tpu_custom_call" | custom-call | flops 12899999744 | bytes 5000000 | tf_op jit(solution)/shard_map/pallas_call | solution.py:397
  120.6 1.8 %copy.11 = f32[6,128,1,128]{3,2,1,0:T(1,128)} copy(f32[6,128,1,128]{3,2,1,0:T(1,128)} %bitcast.6) | data formatting | bytes 786432
